TPU v7x, 256 devices: a whole 4x4x8 slice. The times are simulated.
256 devices in a mesh: kb: 16 (over z, core), pb: 16 (over y, x).
Axes of the slice: x: 4, y: 4, z: 8, core: 2. Of those that a mesh axis runs over, the one named last changes fastest.
Arguments:
- screened: bfloat16 [16, 2, 2048, 2048], P('pb', None, 'kb'), may hold values from -0.09375 to 0.09375
- elem_val: bfloat16 [96, 16, 2, 64, 2048], P('kb', 'pb'), may hold values from -6 to 6
- elem_cond: bfloat16 [96, 16, 2, 64, 2048], P('kb', 'pb'), may hold values from -0.09375 to 0.09375
- pair_first: int32 [96, 16], P('kb', 'pb'), may hold values from 0 to 63, as said below
- pair_second: int32 [96, 16], P('kb', 'pb'), may hold values from 0 to 63, as said below
- coeffs: float32 [64, 2], P('kb'), may hold values from -6 to 6
Outputs:
- kernel_applied: float32 [64, 2, 4096], P('kb', None, 'pb')
Inputs may be any that keep to these rules, and one draw needn't show every extreme that they name: `pair_first`: slot rows s with s // 6 = b hold first k points in b * 4 to (b + 1) * 4 - 1. Each pair lies in the Hermitian half: pair_second is at least pair_first.
All inputs are finite; a program needn't handle non-finite values.
Results may differ from a plain program's by a relative error of at most 0.0029.
Values may be sent and summed in bfloat16 or wider, within the bound.
A program may use at most 192 MiB of HBM per device.

v0:
```python
import jax
import jax.numpy as jnp
from jax import lax
from jax.sharding import PartitionSpec as P


def screened_apply(weights, values):
    real_part = jnp.einsum(
        "gh,pvh->pgv", weights[0], values[:, 0], preferred_element_type=jnp.float32
    ) - jnp.einsum("gh,pvh->pgv", weights[1], values[:, 1], preferred_element_type=jnp.float32)
    imag_part = jnp.einsum(
        "gh,pvh->pgv", weights[0], values[:, 1], preferred_element_type=jnp.float32
    ) + jnp.einsum("gh,pvh->pgv", weights[1], values[:, 0], preferred_element_type=jnp.float32)
    return (real_part.astype(jnp.bfloat16), imag_part.astype(jnp.bfloat16))


def kernel_blocks(conds, real_part, imag_part):
    cond_re = conds[:, 0]
    cond_im = conds[:, 1]
    block_re = jnp.einsum(
        "pcg,pgv->pcv", cond_re, real_part, preferred_element_type=jnp.float32
    ) + jnp.einsum("pcg,pgv->pcv", cond_im, imag_part, preferred_element_type=jnp.float32)
    block_im = jnp.einsum(
        "pcg,pgv->pcv", cond_re, imag_part, preferred_element_type=jnp.float32
    ) - jnp.einsum("pcg,pgv->pcv", cond_im, real_part, preferred_element_type=jnp.float32)
    return jnp.stack((block_re, block_im), axis=1)


def body(screened, elem_val, elem_cond, pair_first, pair_second, coeffs):
    values = elem_val[:, 0]
    conds = elem_cond[:, 0]
    slots = values.shape[0]
    real_part, imag_part = screened_apply(
        lax.all_gather(screened, "kb", axis=2, tiled=True)[0], values
    )
    blocks = kernel_blocks(conds, real_part, imag_part)
    table = lax.all_gather(coeffs, "kb", axis=0, tiled=True)
    count_k = table.shape[0]
    partner = pair_second[:, 0]
    pick = (partner[:, None] == jnp.arange(count_k, dtype=jnp.int32)[None, :]).astype(jnp.float32)
    chosen = jnp.dot(pick, table, precision=lax.Precision.HIGHEST)
    coef_re = chosen[:, 0][:, None, None]
    coef_im = chosen[:, 1][:, None, None]
    term_re = blocks[:, 0] * coef_re - blocks[:, 1] * coef_im
    term_im = blocks[:, 0] * coef_im + blocks[:, 1] * coef_re
    terms = jnp.stack((term_re, term_im), axis=1).reshape(slots, 2, -1)
    local_k = coeffs.shape[0]
    offset = lax.axis_index("kb") * local_k
    owner = pair_first[:, 0] - offset
    select = (jnp.arange(local_k, dtype=jnp.int32)[:, None] == owner[None, :]).astype(jnp.float32)
    summed = jnp.einsum("kp,pxy->kxy", select, terms, precision=lax.Precision.HIGHEST)
    return lax.psum_scatter(summed, "pb", scatter_dimension=2, tiled=True)


def solution(mesh):
    in_specs = (
        P("pb", None, "kb", None),
        P("kb", "pb", None, None, None),
        P("kb", "pb", None, None, None),
        P("kb", "pb"),
        P("kb", "pb"),
        P("kb", None),
    )
    out_specs = P("kb", None, "pb")
    return jax.shard_map(body, mesh=mesh, in_specs=in_specs, out_specs=out_specs, check_vma=False)
```

profile of v0, /device:TPU:1, one launch (start us, length us, event | category | flops | bytes accessed | tf_op | source)
XLA Modules:
  0.0 233.0 jit_solution(6762156641362532423)
XLA Ops:
  6.5 0.0 all-gather.3.cloned.1.call-start
  6.5 0.7 all-gather.3.cloned.1.call-update
  7.3 0.0 reduce-scatter.4.cloned.1.call-start
  7.3 21.5 %all-gather = f32[16,4,2]{1,2,0:T(2,128)S(1)} all-gather(f32[1,4,2]{1,2,0:T(2,128)} %bitcast.79), channel_id=1, replica_groups=mesh['kb'=16,'pb'=16] {'kb'}, dimensions={0}, use_global_device_ids=true | all-gather | bytes 544 | tf_op jit(solution)/shard_map/all_gather | solution.py:37
  28.9 0.1 reshape.19
  28.9 0.0 copy-start
  29.0 4.1 %copy.29 = bf16[6,1,2,64,2048]{4,3,0,2,1:T(8,128)(2,1)} copy(bf16[6,1,2,64,2048]{4,3,2,1,0:T(8,128)(2,1)} %param.7) | data formatting | bytes 6291456 | tf_op args[1]
  33.0 0.0 copy-done
  33.1 0.0 copy-start.2
  33.1 0.0 copy-start.3
  33.1 0.2 copy.28
  33.3 0.4 copy-done.2
  33.7 0.0 copy-done.3
  33.7 0.2 fusion.14
  33.9 75.0 %all-gather.3.cloned.1.call-done = bf16[1,2,2048,2048]{3,2,1,0:T(8,128)(2,1)} async-done(((bf16[1,2,128,2048]{3,2,1,0:T(8,128)(2,1)}), bf16[1,2,2048,2048]{3,2,1,0:T(8,128)(2,1)}) %all-gather.3.cloned.1.call-update) | async-done | bytes 16777232 | tf_op jit(solution)/shard_map/all_gather | solution.py:34
  108.9 0.0 copy-start.1
  108.9 6.5 %fusion = f32[6,64,2048]{2,1,0:T(8,128)S(1)} fusion(bf16[1,2,2048,2048]{3,2,1,0:T(8,128)(2,1)} %all-gather.3.cloned.1.call-done, bf16[6,2,64,2048]{3,2,0,1:T(8,128)(2,1)} %bitcast.74), kind=kOutput, calls=%fused_computation.2 | convolution fusion | flops 3221225472 | bytes 13107200 | tf_op jit(solution)/shard_map/gh,pvh->pgv/dot_general | solution.py:11
  115.4 0.0 copy-done.1
  115.4 6.9 %add_convert_fusion = bf16[6,64,2048]{2,1,0:T(8,128)(2,1)S(1)} fusion(f32[6,64,2048]{2,1,0:T(8,128)S(1)} %fusion, bf16[1,2,2048,2048]{3,2,1,0:T(8,128)(2,1)} %all-gather.3.cloned.1.call-done, bf16[6,2,64,2048]{3,2,0,1:T(8,128)(2,1)S(1)} %bitcast.75), kind=kOutput, calls=%fused_computation.8 | convolution fusion | flops 3222798336 | bytes 14680064 | tf_op jit(solution)/shard_map/gh,pvh->pgv/dot_general | solution.py:13
  122.3 0.7 fusion.4
  123.0 5.9 %fusion.1 = f32[6,64,2048]{2,1,0:T(8,128)S(1)} fusion(bf16[1,2,2048,2048]{3,2,1,0:T(8,128)(2,1)} %all-gather.3.cloned.1.call-done, bf16[6,2,64,2048]{3,2,0,1:T(8,128)(2,1)S(1)} %bitcast.76), kind=kOutput, calls=%fused_computation.3 | convolution fusion | flops 3221225472 | bytes 13107200 | tf_op jit(solution)/shard_map/gh,pvh->pgv/dot_general | solution.py:8
  128.9 6.9 %subtract_convert_fusion = bf16[6,64,2048]{2,1,0:T(8,128)(2,1)S(1)} fusion(f32[6,64,2048]{2,1,0:T(8,128)S(1)} %fusion.1, bf16[1,2,2048,2048]{3,2,1,0:T(8,128)(2,1)} %all-gather.3.cloned.1.call-done, bf16[6,2,64,2048]{3,2,0,1:T(8,128)(2,1)S(1)} %bitcast.77), kind=kOutput, calls=%fused_computation.9 | convolution fusion | flops 3222798336 | bytes 14680064 | tf_op jit(solution)/shard_map/gh,pvh->pgv/dot_general | solution.py:10
  135.7 0.7 fusion.5
  136.4 0.6 fusion.8
  137.1 0.7 subtract_bitcast_fusion
  137.8 0.1 copy.20
  137.9 0.1 stack.9
  138.0 0.1 copy.21
  138.1 0.1 stack.10
  138.3 0.3 fusion.10
  138.5 4.4 %copy.23 = f32[4,2,4096]{0,1,2:T(2,128)} copy(f32[4,2,4096]{2,0,1:T(4,128)S(1)} %fusion.10) | data formatting | bytes 262144
  142.9 5.4 %reshape.23 = f32[4096,8]{1,0:T(8,128)} reshape(f32[4096,2,4]{2,1,0:T(2,128)} %bitcast.69) | data formatting | bytes 262144
  148.3 0.0 reduce-scatter.4.cloned.1.call-update
  148.3 76.1 %reduce-scatter.4.cloned.1.call-done = f32[256,8]{1,0:T(8,128)} async-done(((f32[4096,8]{1,0:T(8,128)}), f32[256,8]{1,0:T(8,128)}) %reduce-scatter.4.cloned.1.call-update) | async-done | bytes 8208
  224.4 1.1 reshape.24
  225.5 0.7 copy.22
  (3 shorter events, 0.0 us)
Async XLA Ops:
  6.5 102.3 %all-gather.3.cloned.1.call-start = ((), (), s32[]{:S(2)}) async-start(), calls=%async_computation.1 | async-start | bytes 17825792 | tf_op jit(solution)/shard_map/all_gather | solution.py:34
  7.3 217.1 %reduce-scatter.4.cloned.1.call-start = ((), (), s32[]{:S(2)}) async-start(), calls=%async_computation.2 | async-start | bytes 2228224
  28.9 4.1 %copy-start = (bf16[6,1,2,64,2048]{4,3,2,1,0:T(8,128)(2,1)S(1)}, bf16[6,1,2,64,2048]{4,3,2,1,0:T(8,128)(2,1)}, u32[]{:S(2)}) copy-start(bf16[6,1,2,64,2048]{4,3,2,1,0:T(8,128)(2,1)} %param.8) | copy-start | bytes 9437188
  33.1 0.7 copy-start.2
  33.1 0.7 copy-start.3
  108.9 6.5 %copy-start.1 = (bf16[6,1,2,64,2048]{4,3,0,2,1:T(8,128)(2,1)S(1)}, bf16[6,1,2,64,2048]{4,3,0,2,1:T(8,128)(2,1)}, u32[]{:S(2)}) copy-start(bf16[6,1,2,64,2048]{4,3,0,2,1:T(8,128)(2,1)} %copy.29) | copy-start | bytes 9437188
Sparse Core Ops, SparseCore 0:
  9.2 99.6 all-gather.2
  148.4 75.9 reduce-scatter.3
where the time goes:
time: 234 us; the launch traced here: 233 us
  waiting for transfers between devices  152 us (65%)
  matrix products  29.3 us (13%)
  blocking collectives  21.5 us (9%)
  local copies, waits for them, and re-layouts  16.9 us (7%)
  between operations  13.5 us (6%)
    unnamed x3, waiting for transfers between devices  76.8 us
    all_gather x1, waiting for transfers between devices, body(): lax.all_gather(screened, 'kb', axis=2, tiled=True)[0]  75 us
    all_gather x1, blocking collectives, body(): table = lax.all_gather(coeffs, 'kb', axis=0, tiled=True)  21.5 us
    unnamed x14, local copies, waits for them, and re-layouts  15.7 us
    dot_general x1, matrix products, screened_apply(): jnp.einsum('gh,pvh->pgv', weights[1], values[:, 1], preferred_element_typ...  6.86 us
    dot_general x1, matrix products, screened_apply(): jnp.einsum('gh,pvh->pgv', weights[1], values[:, 0], preferred_element_typ...  6.86 us
    dot_general x1, matrix products, screened_apply(): jnp.einsum('gh,pvh->pgv', weights[0], values[:, 1], preferred_element_typ...  6.5 us
    dot_general x1, matrix products, screened_apply(): jnp.einsum('gh,pvh->pgv', weights[0], values[:, 0], preferred_element_typ...  5.88 us
  transfers between devices with their start and end apart: 2, of which 2 were waited for; matrix products, arithmetic and copies ran while one was open for 2% of the time, Pallas kernels for 0%

commit v1 on v0

v1 whole, which is shorter than its diff:
```python
import functools

import jax
import jax.numpy as jnp
from jax import lax
from jax.experimental import pallas as pl
from jax.experimental.pallas import tpu as pltpu
from jax.sharding import PartitionSpec as P

MESH = pl.DeviceIdType.MESH
CHUNKS = 4
UP, DOWN = 0, 1


def kernel(
    ring, transfers, w_hbm, val_hbm, cond_hbm, first_ref, second_ref, coef_ref, out_ref,
    w_all, val, val_t, cond, image, acc, table, picked, stage, landed,
    local_sem, ring_send, ring_recv, pair_send, pair_recv, own_send, own_recv,
    coef_send, coef_recv, coef_pair_send, coef_pair_recv, sum_send, sum_recv,
):
    half = ring // 2
    rows = w_hbm.shape[2]
    chunk = rows // CHUNKS
    slots = cond.shape[0]
    local_k = coef_ref.shape[1]
    bands = cond.shape[1] // 2
    kb, pb = lax.axis_index("kb"), lax.axis_index("pb")
    z, core = kb // 2, kb % 2
    sibling = kb + 1 - 2 * core
    up = lax.rem(z + 1, ring) * 2 + core
    down = lax.rem(z + ring - 1, ring) * 2 + core

    def level(direction, hop):
        return lax.rem(z + ring - hop, ring) if direction == UP else lax.rem(z + hop, ring)

    def piece(block, index):
        return w_all.at[block, :, pl.ds(pl.multiple_of(index * chunk, chunk), chunk), :]

    def ring_out(direction, hop, index):
        block = 2 * level(direction, hop - 1) + core
        if isinstance(hop, int) and hop == 1:
            src = w_hbm.at[0, :, pl.ds(index * chunk, chunk), :]
        else:
            src = piece(block, index)
        place = (hop - 1) * CHUNKS + index
        return pltpu.make_async_remote_copy(
            src_ref=src, dst_ref=piece(block, index),
            send_sem=ring_send.at[direction, place], recv_sem=ring_recv.at[direction, place],
            device_id={"kb": up if direction == UP else down}, device_id_type=MESH,
        )

    def ring_in(direction, hop, index):
        block = 2 * level(direction, hop) + core
        place = (hop - 1) * CHUNKS + index
        return pltpu.make_async_remote_copy(
            src_ref=piece(block, index), dst_ref=piece(block, index),
            send_sem=ring_send.at[direction, place], recv_sem=ring_recv.at[direction, place],
            device_id={"kb": up if direction == UP else down}, device_id_type=MESH,
        )

    def pair(direction, hop, index, owner):
        block = 2 * level(direction, hop) + owner
        place = (hop - 1) * CHUNKS + index
        return pltpu.make_async_remote_copy(
            src_ref=piece(block, index), dst_ref=piece(block, index),
            send_sem=pair_send.at[direction, place], recv_sem=pair_recv.at[direction, place],
            device_id={"kb": sibling}, device_id_type=MESH,
        )

    def own_pair(owner):
        return pltpu.make_async_remote_copy(
            src_ref=w_hbm.at[0], dst_ref=w_all.at[owner], send_sem=own_send, recv_sem=own_recv,
            device_id={"kb": sibling}, device_id_type=MESH,
        )

    def coef_pair(owner):
        return pltpu.make_async_remote_copy(
            src_ref=table.at[owner], dst_ref=table.at[owner], send_sem=coef_pair_send, recv_sem=coef_pair_recv,
            device_id={"kb": sibling}, device_id_type=MESH,
        )

    def coef_ring(direction, hop, at):
        both = table.at[pl.ds(2 * at, 2)]
        return pltpu.make_async_remote_copy(
            src_ref=both, dst_ref=both,
            send_sem=coef_send.at[direction, hop - 1], recv_sem=coef_recv.at[direction, hop - 1],
            device_id={"kb": up if direction == UP else down}, device_id_type=MESH,
        )

    def partial_sum(distance):
        return pltpu.make_async_remote_copy(
            src_ref=stage.at[lax.rem(pb + distance, transfers)], dst_ref=landed.at[distance],
            send_sem=sum_send.at[distance], recv_sem=sum_recv.at[distance],
            device_id={"pb": lax.rem(pb + distance, transfers)}, device_id_type=MESH,
        )

    lane = lax.broadcasted_iota(jnp.int32, (1, 2 * bands), 1)
    minus_plus = jnp.where(lane < bands, -1.0, 1.0)

    def turn(block):
        return pltpu.roll(block, bands, axis=1) * minus_plus

    def make_image(pieces):
        rows_in = jnp.concatenate(
            [
                w_all[block, part, pl.ds(pl.multiple_of(index * chunk, chunk), chunk), :]
                for block, index, _, _ in pieces
                for part in range(2)
            ],
            axis=0,
        )
        for pair_of in range(slots // 2):
            wide = slice(pair_of * 4 * bands, (pair_of + 1) * 4 * bands)
            product = jnp.dot(rows_in, val_t[:, wide], preferred_element_type=jnp.float32)
            for i, (_, _, buffer, row) in enumerate(pieces):
                by_real = product[2 * i * chunk : (2 * i + 1) * chunk]
                by_imag = product[(2 * i + 1) * chunk : (2 * i + 2) * chunk]
                for s in range(2):
                    lanes = slice(s * 2 * bands, (s + 1) * 2 * bands)
                    to = (pair_of * 2 + s) * 2 * bands
                    image[buffer, pl.ds(pl.multiple_of(row, chunk), chunk), to : to + 2 * bands] = (
                        by_real[:, lanes] + turn(by_imag[:, lanes])
                    ).astype(jnp.bfloat16)

    def make_blocks(at, buffer):
        columns = pl.ds(pl.multiple_of(at * 2 * rows, 2 * rows), 2 * rows)
        for s in range(slots):
            acc[s] += jnp.dot(
                cond[s, :, columns],
                image[buffer, :, s * 2 * bands : (s + 1) * 2 * bands],
                preferred_element_type=jnp.float32,
            )

    loads = [
        pltpu.make_async_copy(val_hbm, val, local_sem.at[0]),
        pltpu.make_async_copy(w_hbm.at[0], w_all.at[kb], local_sem.at[1]),
        pltpu.make_async_copy(cond_hbm, cond, local_sem.at[2]),
    ]
    for load in loads:
        load.start()

    barrier = pltpu.get_barrier_semaphore()
    for other in (up, down, sibling):
        pl.semaphore_signal(barrier, inc=1, device_id={"kb": other}, device_id_type=MESH)
    for distance in range(1, transfers):
        pl.semaphore_signal(
            barrier, inc=1, device_id={"pb": lax.rem(pb + distance, transfers)}, device_id_type=MESH
        )
    pl.semaphore_wait(barrier, 3 + transfers - 1)

    for index in range(CHUNKS):
        ring_out(UP, 1, index).start()
        ring_out(DOWN, 1, CHUNKS - 1 - index).start()
    own_pair(kb).start()

    table[kb] = jnp.zeros_like(table[0])
    table[kb, 0:2, 0:local_k] = coef_ref[...]
    coef_pair(kb).start()
    acc[...] = jnp.zeros_like(acc)
    loads[0].wait()
    for k in range(val.shape[1] // 256):
        val_t[k * 256 : (k + 1) * 256, :] = val[:, k * 256 : (k + 1) * 256].T
    coef_pair(sibling).wait_recv()
    coef_ring(UP, 1, z).start()
    coef_ring(DOWN, 1, z).start()
    loads[1].wait()
    own_pair(sibling).wait_recv()

    def own_step(step, carry):
        make_image([
            (2 * z + owner, 2 * step + i, 0, owner * rows + (2 * step + i) * chunk)
            for i in range(2) for owner in range(2)
        ])
        return carry

    lax.fori_loop(0, CHUNKS // 2, own_step, 0)
    loads[2].wait()
    make_blocks(z, 0)

    def ring_step(step, carry):
        hop, index = step // CHUNKS + 1, step % CHUNKS
        ring_in(UP, hop, index).wait_recv()

        @pl.when((hop < half - 1) | (index < CHUNKS // 2))
        def _():
            ring_out(UP, hop + 1, index).start()

        pair(UP, hop, index, core).start()
        ring_in(DOWN, hop, CHUNKS - 1 - index).wait_recv()

        @pl.when((hop < half - 1) | (index < CHUNKS // 2))
        def _():
            ring_out(DOWN, hop + 1, CHUNKS - 1 - index).start()

        pair(DOWN, hop, CHUNKS - 1 - index, core).start()

        @pl.when(index == 0)
        def _():
            coef_ring(UP, hop, level(UP, hop)).wait_recv()
            coef_ring(UP, hop + 1, level(UP, hop)).start()
            coef_ring(DOWN, hop, level(DOWN, hop)).wait_recv()

            @pl.when(hop < half - 1)
            def _():
                coef_ring(DOWN, hop + 1, level(DOWN, hop)).start()

        pair(UP, hop, index, 1 - core).wait_recv()
        pair(DOWN, hop, CHUNKS - 1 - index, 1 - core).wait_recv()
        make_image([
            (2 * level(direction, hop) + owner, at, direction, owner * rows + at * chunk)
            for direction, at in ((UP, index), (DOWN, CHUNKS - 1 - index))
            for owner in range(2)
        ])

        @pl.when(index == CHUNKS - 1)
        def _():
            make_blocks(level(UP, hop), UP)
            make_blocks(level(DOWN, hop), DOWN)

        return carry

    lax.fori_loop(0, (half - 1) * CHUNKS, ring_step, 0)

    own_pair(kb).wait_send()
    coef_pair(kb).wait_send()

    def sent_step(step, carry):
        hop, index = step // CHUNKS + 1, step % CHUNKS
        for direction in (UP, DOWN):
            ring_in(direction, hop, index).wait_send()
            pair(direction, hop, index, core).wait_send()
        return carry

    lax.fori_loop(0, (half - 1) * CHUNKS, sent_step, 0)
    for hop in range(1, half):
        for direction in (UP, DOWN):
            coef_ring(direction, hop, z).wait_send()
    coef_ring(UP, half, z).wait_send()
    coef_ring(UP, half, level(UP, half)).wait_recv()

    where_block = lax.broadcasted_iota(jnp.int32, table.shape, 0)
    where_lane = lax.broadcasted_iota(jnp.int32, table.shape, 2)
    point = jnp.where(where_lane < local_k, where_block * local_k + where_lane, -1)
    coefs = table[...]
    for s in range(slots):
        chosen = jnp.sum(jnp.where(point == second_ref[0, s], coefs, 0.0), axis=0)
        chosen = jnp.sum(chosen, axis=1, keepdims=True)
        picked[2 * s : 2 * s + 2, :] = jnp.broadcast_to(chosen[0:2, :], (2, picked.shape[1]))

    def last_step(index, carry):
        ring_in(UP, half, index).wait_recv()
        pair(UP, half, index, core).start()
        ring_in(DOWN, half, CHUNKS - 1 - index).wait_recv()
        pair(DOWN, half, CHUNKS - 1 - index, core).start()
        pair(UP, half, index, 1 - core).wait_recv()
        pair(DOWN, half, CHUNKS - 1 - index, 1 - core).wait_recv()
        make_image([
            (2 * level(UP, half) + owner, at, 0, owner * rows + at * chunk)
            for at in (index, CHUNKS - 1 - index)
            for owner in range(2)
        ])
        return carry

    lax.fori_loop(0, CHUNKS // 2, last_step, 0)
    make_blocks(level(UP, half), 0)

    totals = [jnp.zeros((bands, 2 * bands), jnp.float32) for _ in range(local_k)]
    for s in range(slots):
        block = acc[s, 0:bands, :] - turn(acc[s, bands:, :])
        term = block * picked[2 * s : 2 * s + 1, :] + turn(block) * picked[2 * s + 1 : 2 * s + 2, :]
        owner = first_ref[0, s] - kb * local_k
        for k in range(local_k):
            totals[k] += jnp.where(owner == k, term, 0.0)
    take = bands // transfers
    for k in range(local_k):
        for to in range(transfers):
            stage[to, k * take : (k + 1) * take, :] = totals[k][to * take : (to + 1) * take, :]
    for distance in range(1, transfers):
        partial_sum(distance).start()
    for index in range(CHUNKS // 2):
        for direction, at in ((UP, index), (DOWN, CHUNKS - 1 - index)):
            ring_in(direction, half, at).wait_send()
            pair(direction, half, at, core).wait_send()
    total = stage[pb]
    for distance in range(1, transfers):
        partial_sum(distance).wait_recv()
        total += landed[distance]
    for k in range(local_k):
        for i in range(take // 2):
            even = total[k * take + 2 * i : k * take + 2 * i + 1, :]
            odd = total[k * take + 2 * i + 1 : k * take + 2 * i + 2, :]
            lanes = slice(i * 2 * bands, (i + 1) * 2 * bands)
            out_ref[k, 0:1, lanes] = jnp.where(lane < bands, even, pltpu.roll(odd, bands, axis=1))
            out_ref[k, 1:2, lanes] = jnp.where(lane < bands, pltpu.roll(even, bands, axis=1), odd)
    for distance in range(1, transfers):
        partial_sum(distance).wait_send()


def body(ring, transfers, screened, elem_val, elem_cond, pair_first, pair_second, coeffs):
    slots, _, _, bands, depth = elem_val.shape
    rows = screened.shape[2]
    local_k = coeffs.shape[0]
    half = ring // 2
    take = bands // transfers
    hbm = pl.BlockSpec(memory_space=pltpu.HBM)
    smem = pl.BlockSpec(memory_space=pltpu.SMEM)
    vmem = pl.BlockSpec(memory_space=pltpu.VMEM)
    dma = pltpu.SemaphoreType.DMA
    width = slots * 2 * bands
    return pl.pallas_call(
        functools.partial(kernel, ring, transfers),
        out_shape=jax.ShapeDtypeStruct((local_k, 2, take * bands), jnp.float32),
        in_specs=[hbm, hbm, hbm, smem, smem, vmem],
        out_specs=vmem,
        scratch_shapes=[
            pltpu.VMEM((2 * ring, 2, rows, depth), jnp.bfloat16),
            pltpu.VMEM((width, depth), jnp.bfloat16),
            pltpu.VMEM((depth, width), jnp.bfloat16),
            pltpu.VMEM((slots, 2 * bands, depth), jnp.bfloat16),
            pltpu.VMEM((2, 2 * rows, width), jnp.bfloat16),
            pltpu.VMEM((slots, 2 * bands, 2 * bands), jnp.float32),
            pltpu.VMEM((2 * ring, 8, 128), jnp.float32),
            pltpu.VMEM((2 * slots, 128), jnp.float32),
            pltpu.VMEM((transfers, local_k * take, 2 * bands), jnp.float32),
            pltpu.VMEM((transfers, local_k * take, 2 * bands), jnp.float32),
            dma((3,)),
            dma((2, half * CHUNKS)),
            dma((2, half * CHUNKS)),
            dma((2, half * CHUNKS)),
            dma((2, half * CHUNKS)),
            dma(()),
            dma(()),
            dma((2, half)),
            dma((2, half)),
            dma(()),
            dma(()),
            dma((transfers,)),
            dma((transfers,)),
        ],
        compiler_params=pltpu.CompilerParams(
            collective_id=0, has_side_effects=True, vmem_limit_bytes=56 * 1024 * 1024
        ),
        cost_estimate=pl.CostEstimate(
            flops=8 * depth * depth * slots * bands, bytes_accessed=8 * 1024 * 1024, transcendentals=0
        ),
    )(
        screened, elem_val.reshape(width, depth), elem_cond.reshape(slots, 2 * bands, depth),
        pair_first.T, pair_second.T, coeffs.T,
    )


def solution(mesh):
    in_specs = (
        P("pb", None, "kb", None),
        P("kb", "pb", None, None, None),
        P("kb", "pb", None, None, None),
        P("kb", "pb"),
        P("kb", "pb"),
        P("kb", None),
    )
    out_specs = P("kb", None, "pb")
    ring, transfers = mesh.shape["kb"] // 2, mesh.shape["pb"]
    return jax.shard_map(
        functools.partial(body, ring, transfers), mesh=mesh, in_specs=in_specs, out_specs=out_specs, check_vma=False
    )
```

time: 234 us -> 103 us (0.44)
  waiting for transfers between devices: 152 us -> 0 us
  Pallas kernels: 0 us -> 102 us
  matrix products: 29.3 us -> 0 us
  blocking collectives: 21.5 us -> 0 us
  local copies, waits for them, and re-layouts: 16.9 us -> 1.3 us
  between operations: 13.5 us -> 0.01 us
    pallas_call x0 -> x1, Pallas kernels: none -> 102 us  [body(): pl.pallas_call(functools.partial(kernel, ring, transfers), out_shape=jax....]
    unnamed x3 -> x0, waiting for transfers between devices: 76.8 us -> none
    all_gather x1 -> x0, waiting for transfers between devices: 75 us -> none  [body(): lax.all_gather(screened, 'kb', axis=2, tiled=True)[0]]
    dot_general x10 -> x0, matrix products: 29.3 us -> none  [the longest x1 6.86 us: screened_apply(): jnp.einsum('gh,pvh->pgv', weights[1], values[:, 1], preferred_element_typ...]
    all_gather x1 -> x0, blocking collectives: 21.5 us -> none  [body(): table = lax.all_gather(coeffs, 'kb', axis=0, tiled=True)]
    unnamed x14 -> x1, local copies, waits for them, and re-layouts: 15.7 us -> 1.3 us
  transfers between devices with their start and end apart: 2 -> 0, of which waited for: 2 -> 0; matrix products, arithmetic and copies ran while one was open for 2% -> 0% of each run, Pallas kernels for 0% -> 0%
where the time goes in v1:
time: 103 us
  Pallas kernels  102 us (99%)
  local copies, waits for them, and re-layouts  1.3 us (1%)
    pallas_call x1, Pallas kernels, body(): pl.pallas_call(functools.partial(kernel, ring, transfers), out_shape=jax....  102 us

profile of v1, /device:TPU:1, one launch (start us, length us, event | category | flops | bytes accessed | tf_op | source)
XLA Modules:
  0.0 103.3 jit_solution(4261819955490135093)
XLA Ops:
  0.0 102.0 %shard_map.64 = f32[4,2,256]{2,1,0:T(2,128)} custom-call(bf16[1,2,128,2048]{3,2,1,0:T(8,128)(2,1)} %w_hbm.1, bf16[768,2048]{1,0:T(8,128)(2,1)} %bitcast.5, bf16[6,128,2048]{2,1,0:T(8,128)(2,1)} %bitcast.6, s32[1,6]{1,0:T(1,128)} %bitcast.8, s32[1,6]{1,0:T(1,128)} %bitcast.9, f32[2,4]{1,0:T(2,128)} %bitcast.7), custom_call_target="tpu_custom_call" | custom-call | flops 12884901888 | bytes 8388608 | tf_op jit(solution)/shard_map/pallas_call | solution.py:310
  102.0 1.3 %copy.8 = f32[4,2,256]{2,1,0:T(2,128)} copy(f32[4,2,256]{2,1,0:T(2,128)} %shard_map.64) | data formatting | bytes 16384

commit v2 on v1

v2 whole, which is shorter than its diff:
```python
import functools

import jax
import jax.numpy as jnp
from jax import lax
from jax.experimental import pallas as pl
from jax.experimental.pallas import tpu as pltpu
from jax.sharding import PartitionSpec as P

MESH = pl.DeviceIdType.MESH
CHUNKS = 4
FLIGHT = 2
UP, DOWN = 0, 1


def side_of(transfers):
    return 1 << ((transfers.bit_length() - 1) // 2)


def rounds_of(transfers):
    side = side_of(transfers)
    return max(side // 2 + transfers // side // 2 - 1, 1)


def kernel(
    ring, transfers, w_hbm, val_hbm, cond_hbm, first_hbm, second_hbm, coef_hbm, out_ref,
    w_all, val, val_t, cond, image, acc, table, picked, stage, landed, first, second, coef,
    local_sem, ring_send, ring_recv, pair_send, pair_recv, own_recv,
    coef_send, coef_recv, coef_pair_recv, sum_send, sum_recv, known,
):
    half = ring // 2
    rows = w_hbm.shape[2]
    chunk = rows // CHUNKS
    slots = cond.shape[0]
    local_k = coef.shape[1]
    bands = cond.shape[1] // 2
    far_first = sorted(range(1, transfers), key=lambda distance: abs(distance - transfers // 2))
    total_sends = half * CHUNKS - CHUNKS // 2
    kb, pb = lax.axis_index("kb"), lax.axis_index("pb")
    z, core = kb // 2, kb % 2
    sibling = kb + 1 - 2 * core
    up = lax.rem(z + 1, ring) * 2 + core
    down = lax.rem(z + ring - 1, ring) * 2 + core

    side = side_of(transfers)
    y, x = pb // side, pb % side
    plane = [
        lax.rem(y + dy, transfers // side) * side + lax.rem(x + dx, side)
        for dy, dx in sorted({
            (1 % (transfers // side), 0), (transfers // side - 1, 0), (0, 1 % side), (0, side - 1)
        } - {(0, 0)})
    ]

    def level(direction, hop):
        return lax.rem(z + ring - hop, ring) if direction == UP else lax.rem(z + hop, ring)

    def place(direction, index):
        return index if direction == UP else CHUNKS - 1 - index

    def piece(block, index):
        return w_all.at[block, :, pl.ds(pl.multiple_of(index * chunk, chunk), chunk), :]

    def ring_copy(direction, number, src_hop):
        hop, index = number // CHUNKS + src_hop, place(direction, number % CHUNKS)
        block = 2 * level(direction, hop) + core
        return pltpu.make_async_remote_copy(
            src_ref=piece(block, index), dst_ref=piece(block, index),
            send_sem=ring_send, recv_sem=ring_recv.at[direction, number],
            device_id={"kb": up if direction == UP else down}, device_id_type=MESH,
        )

    def first_copy(direction, number):
        index = place(direction, number)
        return pltpu.make_async_remote_copy(
            src_ref=w_hbm.at[0, :, pl.ds(index * chunk, chunk), :], dst_ref=piece(kb, index),
            send_sem=ring_send, recv_sem=ring_recv.at[direction, number],
            device_id={"kb": up if direction == UP else down}, device_id_type=MESH,
        )

    def pair(direction, number, owner):
        hop, index = number // CHUNKS + 1, place(direction, number % CHUNKS)
        block = 2 * level(direction, hop) + owner
        return pltpu.make_async_remote_copy(
            src_ref=piece(block, index), dst_ref=piece(block, index),
            send_sem=pair_send, recv_sem=pair_recv.at[number],
            device_id={"kb": sibling}, device_id_type=MESH,
        )

    def remote(src, dst, send_sem, recv_sem, device):
        return pltpu.make_async_remote_copy(
            src_ref=src, dst_ref=dst, send_sem=send_sem, recv_sem=recv_sem, device_id=device, device_id_type=MESH
        )

    def arrived(ref, sem):
        pltpu.make_async_copy(ref, ref, sem).wait()

    def own_pair(owner):
        return remote(w_hbm.at[0], w_all.at[owner], pair_send, own_recv, {"kb": sibling})

    def coef_pair(owner):
        return remote(table.at[owner], table.at[owner], coef_send, coef_pair_recv, {"kb": sibling})

    def coef_ring(direction, hop, at):
        both = table.at[pl.ds(2 * at, 2)]
        return remote(
            both, both, coef_send, coef_recv.at[direction, hop - 1], {"kb": up if direction == UP else down}
        )

    lane = lax.broadcasted_iota(jnp.int32, (1, 2 * bands), 1)
    minus_plus = jnp.where(lane < bands, -1.0, 1.0)

    def turn(block):
        return pltpu.roll(block, bands, axis=1) * minus_plus

    def make_image(pieces):
        rows_in = jnp.concatenate(
            [
                w_all[block, part, pl.ds(pl.multiple_of(index * chunk, chunk), chunk), :]
                for block, index, _, _ in pieces
                for part in range(2)
            ],
            axis=0,
        )
        for pair_of in range(slots // 2):
            wide = slice(pair_of * 4 * bands, (pair_of + 1) * 4 * bands)
            product = jnp.dot(rows_in, val_t[:, wide], preferred_element_type=jnp.float32)
            for i, (_, _, buffer, row) in enumerate(pieces):
                by_real = product[2 * i * chunk : (2 * i + 1) * chunk]
                by_imag = product[(2 * i + 1) * chunk : (2 * i + 2) * chunk]
                for s in range(2):
                    lanes = slice(s * 2 * bands, (s + 1) * 2 * bands)
                    to = (pair_of * 2 + s) * 2 * bands
                    image[buffer, pl.ds(pl.multiple_of(row, chunk), chunk), to : to + 2 * bands] = (
                        by_real[:, lanes] + turn(by_imag[:, lanes])
                    ).astype(jnp.bfloat16)

    def make_blocks(at, buffer):
        columns = pl.ds(pl.multiple_of(at * 2 * rows, 2 * rows), 2 * rows)
        for s in range(slots):
            acc[s] += jnp.dot(
                cond[s, :, columns],
                image[buffer, :, s * 2 * bands : (s + 1) * 2 * bands],
                preferred_element_type=jnp.float32,
            )

    loads = [
        pltpu.make_async_copy(src, dst, local_sem.at[i])
        for i, (src, dst) in enumerate((
            (coef_hbm, coef), (val_hbm, val), (w_hbm.at[0], w_all.at[kb]), (cond_hbm, cond),
            (first_hbm, first), (second_hbm, second),
        ))
    ]
    barrier = pltpu.get_barrier_semaphore()
    for other in (up, down, sibling):
        pl.semaphore_signal(barrier, inc=1, device_id={"kb": other}, device_id_type=MESH)
    for other in plane:
        pl.semaphore_signal(barrier, inc=1, device_id={"pb": other}, device_id_type=MESH)
    pl.semaphore_wait(barrier, 3 + len(plane))

    for number in range(FLIGHT):
        first_copy(UP, number).start()
        first_copy(DOWN, number).start()
    own_pair(kb).start()
    for load in loads:
        load.start()

    table[kb] = jnp.zeros_like(table[0])
    loads[0].wait()
    table[kb, 0:2, 0:local_k] = coef[...]
    coef_pair(kb).start()
    acc[...] = jnp.zeros_like(acc)
    loads[1].wait()

    def transpose(k, carry):
        columns = pl.ds(pl.multiple_of(k * 256, 256), 256)
        val_t[columns, :] = val[:, columns].T
        return carry

    lax.fori_loop(0, val.shape[1] // 256, transpose, 0)
    coef_pair(sibling).wait_recv()
    coef_ring(UP, 1, z).start()
    coef_ring(DOWN, 1, z).start()
    for load in loads[2:]:
        load.wait()
    own_pair(sibling).wait_recv()

    def step(at, carry):
        hop, index = at // CHUNKS, at % CHUNKS
        number = at - CHUNKS

        @pl.when(hop > 0)
        def _():
            later = number + FLIGHT
            for direction in (UP, DOWN):
                ring_copy(direction, number, 1).wait_recv()
                pl.when(later < total_sends)(lambda direction=direction: ring_copy(direction, later, 0).start())
                pair(direction, number, core).start()

        @pl.when((hop > 0) & (index == 1) & (hop <= rounds_of(transfers)))
        def _():
            for other in plane:
                pl.semaphore_signal(known.at[hop - 1], inc=1, device_id={"pb": other}, device_id_type=MESH)

        @pl.when((hop > 0) & (index == CHUNKS - 1) & (hop <= rounds_of(transfers)))
        def _():
            pl.semaphore_wait(known.at[hop - 1], len(plane))

        @pl.when((hop > 0) & (index == 0))
        def _():
            coef_ring(UP, hop, level(UP, hop)).wait_recv()

            @pl.when(hop < half)
            def _():
                coef_ring(UP, hop + 1, level(UP, hop)).start()
                coef_ring(DOWN, hop, level(DOWN, hop)).wait_recv()

            @pl.when(hop < half - 1)
            def _():
                coef_ring(DOWN, hop + 1, level(DOWN, hop)).start()

            @pl.when(hop == half)
            def _():
                where_block = lax.broadcasted_iota(jnp.int32, table.shape, 0)
                where_lane = lax.broadcasted_iota(jnp.int32, table.shape, 2)
                point = jnp.where(where_lane < local_k, where_block * local_k + where_lane, -1)
                coefs = table[...]
                for s in range(slots):
                    chosen = jnp.sum(jnp.where(point == second[0, s], coefs, 0.0), axis=0)
                    chosen = jnp.sum(chosen, axis=1, keepdims=True)
                    picked[2 * s : 2 * s + 2, :] = jnp.broadcast_to(chosen[0:2, :], (2, picked.shape[1]))

        @pl.when(hop > 0)
        def _():
            arrived(w_all.at[pl.ds(0, 2), :, pl.ds(0, chunk), :], pair_recv.at[number])

        between = (hop > 0) & (hop < half)
        make_image([
            (2 * level(direction, hop) + owner, at_row, buffer, owner * rows + at_row * chunk)
            for direction, at_row, buffer in (
                (UP, place(UP, index), 0), (DOWN, place(DOWN, index), jnp.where(between, 1, 0)),
            )
            for owner in range(2)
        ])

        @pl.when(index == jnp.where(hop == half, CHUNKS // 2 - 1, CHUNKS - 1))
        def _():
            def blocks(buffer, carry):
                make_blocks(jnp.where(buffer == 0, level(UP, hop), level(DOWN, hop)), buffer)
                return carry

            lax.fori_loop(0, jnp.where(between, 2, 1), blocks, 0)

        return carry

    lax.fori_loop(CHUNKS // 2, half * CHUNKS + CHUNKS // 2, step, 0)

    totals = [jnp.zeros((bands, 2 * bands), jnp.float32) for _ in range(local_k)]
    for s in range(slots):
        block = acc[s, 0:bands, :] - turn(acc[s, bands:, :])
        term = block * picked[2 * s : 2 * s + 1, :] + turn(block) * picked[2 * s + 1 : 2 * s + 2, :]
        owner = first[0, s] - kb * local_k
        for k in range(local_k):
            totals[k] += jnp.where(owner == k, term, 0.0)
    take = bands // transfers
    for k in range(local_k):
        for to in range(transfers):
            stage[to, k * take : (k + 1) * take, :] = totals[k][to * take : (to + 1) * take, :]
    for i, distance in enumerate(far_first):
        to = lax.rem(pb + distance, transfers)
        remote(stage.at[to], landed.at[i], sum_send, sum_recv, {"pb": to}).start()
    arrived(w_all.at[pl.ds(0, ring - 1)], ring_send)
    arrived(w_all.at[pl.ds(0, ring)], pair_send)
    arrived(table.at[pl.ds(0, 1 + 2 * (2 * half - 1))], coef_send)
    total = stage[pb]
    arrived(landed.at[pl.ds(0, transfers - 1)], sum_recv)
    for i in range(transfers - 1):
        total += landed[i]
    for k in range(local_k):
        for i in range(take // 2):
            even = total[k * take + 2 * i : k * take + 2 * i + 1, :]
            odd = total[k * take + 2 * i + 1 : k * take + 2 * i + 2, :]
            lanes = slice(i * 2 * bands, (i + 1) * 2 * bands)
            out_ref[k, 0:1, lanes] = jnp.where(lane < bands, even, pltpu.roll(odd, bands, axis=1))
            out_ref[k, 1:2, lanes] = jnp.where(lane < bands, pltpu.roll(even, bands, axis=1), odd)
    arrived(landed.at[pl.ds(0, transfers - 1)], sum_send)


def body(ring, transfers, screened, elem_val, elem_cond, pair_first, pair_second, coeffs):
    slots, _, _, bands, depth = elem_val.shape
    rows = screened.shape[2]
    local_k = coeffs.shape[0]
    half = ring // 2
    take = bands // transfers
    dma = pltpu.SemaphoreType.DMA
    width = slots * 2 * bands
    return pl.pallas_call(
        functools.partial(kernel, ring, transfers),
        out_shape=jax.ShapeDtypeStruct((local_k, 2, take * bands), jnp.float32),
        in_specs=[pl.BlockSpec(memory_space=pltpu.HBM)] * 6,
        out_specs=pl.BlockSpec(memory_space=pltpu.VMEM),
        scratch_shapes=[
            pltpu.VMEM((2 * ring, 2, rows, depth), jnp.bfloat16),
            pltpu.VMEM((width, depth), jnp.bfloat16),
            pltpu.VMEM((depth, width), jnp.bfloat16),
            pltpu.VMEM((slots, 2 * bands, depth), jnp.bfloat16),
            pltpu.VMEM((2, 2 * rows, width), jnp.bfloat16),
            pltpu.VMEM((slots, 2 * bands, 2 * bands), jnp.float32),
            pltpu.VMEM((2 * ring, 8, 128), jnp.float32),
            pltpu.VMEM((2 * slots, 128), jnp.float32),
            pltpu.VMEM((transfers, local_k * take, 2 * bands), jnp.float32),
            pltpu.VMEM((transfers, local_k * take, 2 * bands), jnp.float32),
            pltpu.SMEM((1, slots), jnp.int32),
            pltpu.SMEM((1, slots), jnp.int32),
            pltpu.VMEM((2, local_k), jnp.float32),
            dma((6,)),
            dma(()),
            dma((2, half * CHUNKS - CHUNKS // 2)),
            dma(()),
            dma((half * CHUNKS - CHUNKS // 2,)),
            dma(()),
            dma(()),
            dma((2, half)),
            dma(()),
            dma(()),
            dma(()),
            pltpu.SemaphoreType.REGULAR((rounds_of(transfers),)),
        ],
        compiler_params=pltpu.CompilerParams(
            collective_id=0, has_side_effects=True, vmem_limit_bytes=40 * 1024 * 1024
        ),
        cost_estimate=pl.CostEstimate(
            flops=8 * depth * depth * slots * bands, bytes_accessed=8 * 1024 * 1024, transcendentals=0
        ),
    )(*(
        pltpu.with_memory_space_constraint(operand, pltpu.HBM)
        for operand in (
            screened, elem_val.reshape(width, depth), elem_cond.reshape(slots, 2 * bands, depth),
            pair_first.T, pair_second.T, coeffs.T,
        )
    ))


def solution(mesh):
    in_specs = (
        P("pb", None, "kb", None),
        P("kb", "pb", None, None, None),
        P("kb", "pb", None, None, None),
        P("kb", "pb"),
        P("kb", "pb"),
        P("kb", None),
    )
    out_specs = P("kb", None, "pb")
    ring, transfers = mesh.shape["kb"] // 2, mesh.shape["pb"]
    return jax.shard_map(
        functools.partial(body, ring, transfers), mesh=mesh, in_specs=in_specs, out_specs=out_specs, check_vma=False
    )
```

time: 103 us -> 99.6 us (0.967)
  Pallas kernels: 102 us -> 98.9 us
    pallas_call x1, Pallas kernels: 102 us -> 98.9 us  [body(): pl.pallas_call(functools.partial(kernel, ring, transfers), out_shape=jax....]
where the time goes in v2:
time: 99.6 us; the launch traced here: 99.5 us
  Pallas kernels  98.9 us (99%)
    pallas_call x1, Pallas kernels, body(): pl.pallas_call(functools.partial(kernel, ring, transfers), out_shape=jax....  98.9 us

profile of v2, /device:TPU:1, one launch (start us, length us, event | category | flops | bytes accessed | tf_op | source)
XLA Modules:
  0.0 99.5 jit_solution(10003070113505616383)
XLA Ops:
  0.0 98.9 %shard_map.64 = f32[4,2,256]{2,1,0:T(2,128)S(1)} custom-call(bf16[1,2,128,2048]{3,2,1,0:T(8,128)(2,1)} %w_hbm.1, bf16[768,2048]{1,0:T(8,128)(2,1)} %bitcast.5, bf16[6,128,2048]{2,1,0:T(8,128)(2,1)} %bitcast.6, s32[1,6]{1,0:T(1,128)} %bitcast.8, s32[1,6]{1,0:T(1,128)} %bitcast.9, f32[2,4]{1,0:T(2,128)} %bitcast.7), custom_call_target="tpu_custom_call" | custom-call | flops 12884901888 | bytes 8388608 | tf_op jit(solution)/shard_map/pallas_call | solution.py:296
  98.9 0.6 copy.8

commit v3 on v2

--- a/solution.py
+++ b/solution.py
@@ -10,6 +10,7 @@
 MESH = pl.DeviceIdType.MESH
 CHUNKS = 4
 FLIGHT = 2
+TAIL = 4
 UP, DOWN = 0, 1
 
 
@@ -35,7 +36,8 @@
     local_k = coef.shape[1]
     bands = cond.shape[1] // 2
     far_first = sorted(range(1, transfers), key=lambda distance: abs(distance - transfers // 2))
-    total_sends = half * CHUNKS - CHUNKS // 2
+    full = (half - 1) * CHUNKS
+    short = rows // 2 // TAIL
     kb, pb = lax.axis_index("kb"), lax.axis_index("pb")
     z, core = kb // 2, kb % 2
     sibling = kb + 1 - 2 * core
@@ -77,6 +79,20 @@
             device_id={"kb": up if direction == UP else down}, device_id_type=MESH,
         )
 
+    def tail_place(direction, at):
+        return pl.multiple_of(at * short if direction == UP else rows - (at + 1) * short, short)
+
+    def tail_copy(direction, at, src_hop):
+        block = 2 * level(direction, half - 1 + src_hop) + core
+        part = w_all.at[block, :, pl.ds(tail_place(direction, at), short), :]
+        return remote(
+            part, part, ring_send, ring_recv.at[direction, full + at], {"kb": up if direction == UP else down}
+        )
+
+    def tail_pair(direction, at):
+        part = w_all.at[2 * level(direction, half) + core, :, pl.ds(tail_place(direction, at), short), :]
+        return remote(part, part, pair_send, pair_recv.at[full + at], {"kb": sibling})
+
     def pair(direction, number, owner):
         hop, index = number // CHUNKS + 1, place(direction, number % CHUNKS)
         block = 2 * level(direction, hop) + owner
@@ -112,11 +128,11 @@
     def turn(block):
         return pltpu.roll(block, bands, axis=1) * minus_plus
 
-    def make_image(pieces):
+    def make_image(size, pieces):
         rows_in = jnp.concatenate(
             [
-                w_all[block, part, pl.ds(pl.multiple_of(index * chunk, chunk), chunk), :]
-                for block, index, _, _ in pieces
+                w_all[block, part, pl.ds(pl.multiple_of(first_row, size), size), :]
+                for block, first_row, _, _ in pieces
                 for part in range(2)
             ],
             axis=0,
@@ -125,12 +141,12 @@
             wide = slice(pair_of * 4 * bands, (pair_of + 1) * 4 * bands)
             product = jnp.dot(rows_in, val_t[:, wide], preferred_element_type=jnp.float32)
             for i, (_, _, buffer, row) in enumerate(pieces):
-                by_real = product[2 * i * chunk : (2 * i + 1) * chunk]
-                by_imag = product[(2 * i + 1) * chunk : (2 * i + 2) * chunk]
+                by_real = product[2 * i * size : (2 * i + 1) * size]
+                by_imag = product[(2 * i + 1) * size : (2 * i + 2) * size]
                 for s in range(2):
                     lanes = slice(s * 2 * bands, (s + 1) * 2 * bands)
                     to = (pair_of * 2 + s) * 2 * bands
-                    image[buffer, pl.ds(pl.multiple_of(row, chunk), chunk), to : to + 2 * bands] = (
+                    image[buffer, pl.ds(pl.multiple_of(row, size), size), to : to + 2 * bands] = (
                         by_real[:, lanes] + turn(by_imag[:, lanes])
                     ).astype(jnp.bfloat16)
 
@@ -187,13 +203,22 @@
     def step(at, carry):
         hop, index = at // CHUNKS, at % CHUNKS
         number = at - CHUNKS
+        later = number + FLIGHT
 
         @pl.when(hop > 0)
         def _():
-            later = number + FLIGHT
             for direction in (UP, DOWN):
                 ring_copy(direction, number, 1).wait_recv()
-                pl.when(later < total_sends)(lambda direction=direction: ring_copy(direction, later, 0).start())
+
+                @pl.when(later < full)
+                def _():
+                    ring_copy(direction, later, 0).start()
+
+                @pl.when((later >= full) & (later < full + CHUNKS // 2))
+                def _():
+                    for i in range(chunk // short):
+                        tail_copy(direction, (later - full) * (chunk // short) + i, 0).start()
+
                 pair(direction, number, core).start()
 
         @pl.when((hop > 0) & (index == 1) & (hop <= rounds_of(transfers)))
@@ -208,51 +233,61 @@
         @pl.when((hop > 0) & (index == 0))
         def _():
             coef_ring(UP, hop, level(UP, hop)).wait_recv()
-
-            @pl.when(hop < half)
-            def _():
-                coef_ring(UP, hop + 1, level(UP, hop)).start()
-                coef_ring(DOWN, hop, level(DOWN, hop)).wait_recv()
+            coef_ring(UP, hop + 1, level(UP, hop)).start()
+            coef_ring(DOWN, hop, level(DOWN, hop)).wait_recv()
 
             @pl.when(hop < half - 1)
             def _():
                 coef_ring(DOWN, hop + 1, level(DOWN, hop)).start()
 
-            @pl.when(hop == half)
-            def _():
-                where_block = lax.broadcasted_iota(jnp.int32, table.shape, 0)
-                where_lane = lax.broadcasted_iota(jnp.int32, table.shape, 2)
-                point = jnp.where(where_lane < local_k, where_block * local_k + where_lane, -1)
-                coefs = table[...]
-                for s in range(slots):
-                    chosen = jnp.sum(jnp.where(point == second[0, s], coefs, 0.0), axis=0)
-                    chosen = jnp.sum(chosen, axis=1, keepdims=True)
-                    picked[2 * s : 2 * s + 2, :] = jnp.broadcast_to(chosen[0:2, :], (2, picked.shape[1]))
-
         @pl.when(hop > 0)
         def _():
             arrived(w_all.at[pl.ds(0, 2), :, pl.ds(0, chunk), :], pair_recv.at[number])
 
-        between = (hop > 0) & (hop < half)
-        make_image([
-            (2 * level(direction, hop) + owner, at_row, buffer, owner * rows + at_row * chunk)
+        make_image(chunk, [
+            (2 * level(direction, hop) + owner, at_row, buffer, owner * rows + at_row)
             for direction, at_row, buffer in (
-                (UP, place(UP, index), 0), (DOWN, place(DOWN, index), jnp.where(between, 1, 0)),
+                (UP, place(UP, index) * chunk, 0), (DOWN, place(DOWN, index) * chunk, jnp.where(hop > 0, 1, 0)),
             )
             for owner in range(2)
         ])
 
-        @pl.when(index == jnp.where(hop == half, CHUNKS // 2 - 1, CHUNKS - 1))
+        @pl.when(index == CHUNKS - 1)
         def _():
             def blocks(buffer, carry):
                 make_blocks(jnp.where(buffer == 0, level(UP, hop), level(DOWN, hop)), buffer)
                 return carry
 
-            lax.fori_loop(0, jnp.where(between, 2, 1), blocks, 0)
+            lax.fori_loop(0, jnp.where(hop > 0, 2, 1), blocks, 0)
 
         return carry
 
-    lax.fori_loop(CHUNKS // 2, half * CHUNKS + CHUNKS // 2, step, 0)
+    lax.fori_loop(CHUNKS // 2, half * CHUNKS, step, 0)
+
+    coef_ring(UP, half, level(UP, half)).wait_recv()
+    where_block = lax.broadcasted_iota(jnp.int32, table.shape, 0)
+    where_lane = lax.broadcasted_iota(jnp.int32, table.shape, 2)
+    point = jnp.where(where_lane < local_k, where_block * local_k + where_lane, -1)
+    coefs = table[...]
+    for s in range(slots):
+        chosen = jnp.sum(jnp.where(point == second[0, s], coefs, 0.0), axis=0)
+        chosen = jnp.sum(chosen, axis=1, keepdims=True)
+        picked[2 * s : 2 * s + 2, :] = jnp.broadcast_to(chosen[0:2, :], (2, picked.shape[1]))
+
+    def last_step(at, carry):
+        for direction in (UP, DOWN):
+            tail_copy(direction, at, 1).wait_recv()
+            tail_pair(direction, at).start()
+        arrived(w_all.at[pl.ds(0, 2), :, pl.ds(0, short), :], pair_recv.at[full + at])
+        make_image(short, [
+            (2 * level(UP, half) + owner, at_row, 0, owner * rows + at_row)
+            for at_row in (tail_place(UP, at), tail_place(DOWN, at))
+            for owner in range(2)
+        ])
+        return carry
+
+    lax.fori_loop(0, TAIL, last_step, 0)
+    make_blocks(level(UP, half), 0)
 
     totals = [jnp.zeros((bands, 2 * bands), jnp.float32) for _ in range(local_k)]
     for s in range(slots):
@@ -314,9 +349,9 @@
             pltpu.VMEM((2, local_k), jnp.float32),
             dma((6,)),
             dma(()),
-            dma((2, half * CHUNKS - CHUNKS // 2)),
-            dma(()),
-            dma((half * CHUNKS - CHUNKS // 2,)),
+            dma((2, (half - 1) * CHUNKS + TAIL)),
+            dma(()),
+            dma(((half - 1) * CHUNKS + TAIL,)),
             dma(()),
             dma(()),
             dma((2, half)),

time: 99.6 us -> 98.8 us (level)
  no operation moved by 1% of the time
where the time goes in v3:
time: 98.8 us
  Pallas kernels  98.1 us (99%)
    pallas_call x1, Pallas kernels, body(): pl.pallas_call(functools.partial(kernel, ring, transfers), out_shape=jax....  98.1 us

profile of v3, /device:TPU:1, one launch (start us, length us, event | category | flops | bytes accessed | tf_op | source)
XLA Modules:
  0.0 98.8 jit_solution(15961094588931673824)
XLA Ops:
  0.0 98.1 %shard_map.64 = f32[4,2,256]{2,1,0:T(2,128)S(1)} custom-call(bf16[1,2,128,2048]{3,2,1,0:T(8,128)(2,1)} %w_hbm.1, bf16[768,2048]{1,0:T(8,128)(2,1)} %bitcast.5, bf16[6,128,2048]{2,1,0:T(8,128)(2,1)} %bitcast.6, s32[1,6]{1,0:T(1,128)} %bitcast.8, s32[1,6]{1,0:T(1,128)} %bitcast.9, f32[2,4]{1,0:T(2,128)} %bitcast.7), custom_call_target="tpu_custom_call" | custom-call | flops 12884901888 | bytes 8388608 | tf_op jit(solution)/shard_map/pallas_call | solution.py:331
  98.2 0.6 copy.8

commit v4 on v3

--- a/solution.py
+++ b/solution.py
@@ -11,6 +11,7 @@
 CHUNKS = 4
 FLIGHT = 2
 TAIL = 4
+DIRECT = 4
 UP, DOWN = 0, 1
 
 
@@ -18,16 +19,16 @@
     return 1 << ((transfers.bit_length() - 1) // 2)
 
 
-def rounds_of(transfers):
+def rounds_of(ring, transfers):
     side = side_of(transfers)
-    return max(side // 2 + transfers // side // 2 - 1, 1)
+    return 2 * (ring // 2) + side // 2 + transfers // side // 2 - 1
 
 
 def kernel(
     ring, transfers, w_hbm, val_hbm, cond_hbm, first_hbm, second_hbm, coef_hbm, out_ref,
     w_all, val, val_t, cond, image, acc, table, picked, stage, landed, first, second, coef,
-    local_sem, ring_send, ring_recv, pair_send, pair_recv, own_recv,
-    coef_send, coef_recv, coef_pair_recv, sum_send, sum_recv, known,
+    local_sem, ring_send, ring_recv, pair_send, pair_recv, own_recv, tail_send, tail_pair_send, end_send, end_recv,
+    coef_send, coef_recv, coef_pair_recv, sum_send, sum_recv, known, joined,
 ):
     half = ring // 2
     rows = w_hbm.shape[2]
@@ -35,7 +36,6 @@
     slots = cond.shape[0]
     local_k = coef.shape[1]
     bands = cond.shape[1] // 2
-    far_first = sorted(range(1, transfers), key=lambda distance: abs(distance - transfers // 2))
     full = (half - 1) * CHUNKS
     short = rows // 2 // TAIL
     kb, pb = lax.axis_index("kb"), lax.axis_index("pb")
@@ -46,12 +46,30 @@
 
     side = side_of(transfers)
     y, x = pb // side, pb % side
-    plane = [
-        lax.rem(y + dy, transfers // side) * side + lax.rem(x + dx, side)
-        for dy, dx in sorted({
-            (1 % (transfers // side), 0), (transfers // side - 1, 0), (0, 1 % side), (0, side - 1)
-        } - {(0, 0)})
-    ]
+    tall = transfers // side
+
+    def hops(dy, dx):
+        return min(dy, tall - dy) + min(dx, side - dx)
+
+    others = sorted(
+        ((dy, dx) for dy in range(tall) for dx in range(side) if dy or dx), key=lambda by: -hops(*by)
+    )
+    others = [(lax.rem(y + dy, tall) * side + lax.rem(x + dx, side), hops(dy, dx)) for dy, dx in others]
+    plane = [other for other, far in others if far == 1]
+
+    rounds = rounds_of(ring, transfers)
+
+    def tell(number):
+        for other in (up, down):
+            pl.semaphore_signal(known.at[number % 2], inc=1, device_id={"kb": other}, device_id_type=MESH)
+
+        @pl.when(z == 0)
+        def _():
+            for other in plane:
+                pl.semaphore_signal(known.at[number % 2], inc=1, device_id={"pb": other}, device_id_type=MESH)
+
+    def hear(number):
+        pl.semaphore_wait(known.at[number % 2], jnp.where(z == 0, 2 + len(plane), 2))
 
     def level(direction, hop):
         return lax.rem(z + ring - hop, ring) if direction == UP else lax.rem(z + hop, ring)
@@ -82,16 +100,26 @@
     def tail_place(direction, at):
         return pl.multiple_of(at * short if direction == UP else rows - (at + 1) * short, short)
 
-    def tail_copy(direction, at, src_hop):
+    depth = w_hbm.shape[3]
+    shared = depth - depth // DIRECT
+
+    def tail_copy(direction, at, src_hop, lanes=depth, send_sem=tail_send.at[0]):
         block = 2 * level(direction, half - 1 + src_hop) + core
-        part = w_all.at[block, :, pl.ds(tail_place(direction, at), short), :]
+        part = w_all.at[block, :, pl.ds(tail_place(direction, at), short), pl.ds(0, lanes)]
         return remote(
-            part, part, ring_send, ring_recv.at[direction, full + at], {"kb": up if direction == UP else down}
-        )
-
-    def tail_pair(direction, at):
-        part = w_all.at[2 * level(direction, half) + core, :, pl.ds(tail_place(direction, at), short), :]
-        return remote(part, part, pair_send, pair_recv.at[full + at], {"kb": sibling})
+            part, part, send_sem, ring_recv.at[direction, full + at], {"kb": up if direction == UP else down}
+        )
+
+    def tail_pair(direction, at, lanes=depth, send_sem=tail_pair_send.at[0]):
+        block = 2 * level(direction, half) + core
+        part = w_all.at[block, :, pl.ds(tail_place(direction, at), short), pl.ds(0, lanes)]
+        return remote(part, part, send_sem, pair_recv.at[full + at], {"kb": sibling})
+
+    def end_copy(direction, to_core):
+        block = 2 * level(direction, half - 1) + core
+        part = w_all.at[block, :, pl.ds(tail_place(direction, TAIL - 1), short), pl.ds(shared, depth - shared)]
+        chip = up - core if direction == UP else down - core
+        return remote(part, part, end_send, end_recv, {"kb": chip + to_core})
 
     def pair(direction, number, owner):
         hop, index = number // CHUNKS + 1, place(direction, number % CHUNKS)
@@ -167,18 +195,25 @@
         ))
     ]
     barrier = pltpu.get_barrier_semaphore()
-    for other in (up, down, sibling):
+    for other in (down, sibling):
         pl.semaphore_signal(barrier, inc=1, device_id={"kb": other}, device_id_type=MESH)
-    for other in plane:
-        pl.semaphore_signal(barrier, inc=1, device_id={"pb": other}, device_id_type=MESH)
-    pl.semaphore_wait(barrier, 3 + len(plane))
-
+
+    @pl.when(z == 0)
+    def _():
+        for other in plane:
+            pl.semaphore_signal(barrier, inc=1, device_id={"pb": other}, device_id_type=MESH)
+
+    pl.semaphore_wait(barrier, jnp.where(z == 0, 2 + len(plane), 2))
+
+    pl.semaphore_signal(joined, inc=1, device_id={"kb": up}, device_id_type=MESH)
     for number in range(FLIGHT):
         first_copy(UP, number).start()
-        first_copy(DOWN, number).start()
     own_pair(kb).start()
     for load in loads:
         load.start()
+    pl.semaphore_wait(joined, 1)
+    for number in range(FLIGHT):
+        first_copy(DOWN, number).start()
 
     table[kb] = jnp.zeros_like(table[0])
     loads[0].wait()
@@ -217,18 +252,27 @@
                 @pl.when((later >= full) & (later < full + CHUNKS // 2))
                 def _():
                     for i in range(chunk // short):
-                        tail_copy(direction, (later - full) * (chunk // short) + i, 0).start()
+                        piece_at = (later - full) * (chunk // short) + i
+
+                        @pl.when(piece_at < TAIL - 1)
+                        def _():
+                            tail_copy(direction, piece_at, 0).start()
+
+                @pl.when(later == full + CHUNKS // 2 - 1)
+                def _():
+                    tail_copy(direction, TAIL - 1, 0, shared, tail_send.at[1]).start()
+                    end_copy(direction, core).start()
+                    end_copy(direction, 1 - core).start()
 
                 pair(direction, number, core).start()
 
-        @pl.when((hop > 0) & (index == 1) & (hop <= rounds_of(transfers)))
-        def _():
-            for other in plane:
-                pl.semaphore_signal(known.at[hop - 1], inc=1, device_id={"pb": other}, device_id_type=MESH)
-
-        @pl.when((hop > 0) & (index == CHUNKS - 1) & (hop <= rounds_of(transfers)))
-        def _():
-            pl.semaphore_wait(known.at[hop - 1], len(plane))
+        @pl.when((number > 0) & (number <= rounds))
+        def _():
+            hear(number - 1)
+
+        @pl.when((number >= 0) & (number < rounds))
+        def _():
+            tell(number)
 
         @pl.when((hop > 0) & (index == 0))
         def _():
@@ -263,6 +307,10 @@
         return carry
 
     lax.fori_loop(CHUNKS // 2, half * CHUNKS, step, 0)
+    for number in range(full, rounds + 1):
+        hear(number - 1)
+        if number < rounds:
+            tell(number)
 
     coef_ring(UP, half, level(UP, half)).wait_recv()
     where_block = lax.broadcasted_iota(jnp.int32, table.shape, 0)
@@ -275,10 +323,21 @@
         picked[2 * s : 2 * s + 2, :] = jnp.broadcast_to(chosen[0:2, :], (2, picked.shape[1]))
 
     def last_step(at, carry):
-        for direction in (UP, DOWN):
-            tail_copy(direction, at, 1).wait_recv()
-            tail_pair(direction, at).start()
-        arrived(w_all.at[pl.ds(0, 2), :, pl.ds(0, short), :], pair_recv.at[full + at])
+        @pl.when(at < TAIL - 1)
+        def _():
+            for direction in (UP, DOWN):
+                tail_copy(direction, at, 1).wait_recv()
+                tail_pair(direction, at).start()
+            arrived(w_all.at[pl.ds(0, 2), :, pl.ds(0, short), :], pair_recv.at[full + at])
+
+        @pl.when(at == TAIL - 1)
+        def _():
+            for direction in (UP, DOWN):
+                tail_copy(direction, TAIL - 1, 1, shared).wait_recv()
+                tail_pair(direction, TAIL - 1, shared, tail_pair_send.at[1]).start()
+            arrived(w_all.at[pl.ds(0, 2), :, pl.ds(0, short), pl.ds(0, shared)], pair_recv.at[full + TAIL - 1])
+            arrived(w_all.at[pl.ds(0, 4), :, pl.ds(0, short), pl.ds(0, depth - shared)], end_recv)
+
         make_image(short, [
             (2 * level(UP, half) + owner, at_row, 0, owner * rows + at_row)
             for at_row in (tail_place(UP, at), tail_place(DOWN, at))
@@ -300,11 +359,14 @@
     for k in range(local_k):
         for to in range(transfers):
             stage[to, k * take : (k + 1) * take, :] = totals[k][to * take : (to + 1) * take, :]
-    for i, distance in enumerate(far_first):
-        to = lax.rem(pb + distance, transfers)
+    for i, (to, _) in enumerate(others):
         remote(stage.at[to], landed.at[i], sum_send, sum_recv, {"pb": to}).start()
-    arrived(w_all.at[pl.ds(0, ring - 1)], ring_send)
-    arrived(w_all.at[pl.ds(0, ring)], pair_send)
+    arrived(w_all.at[pl.ds(0, ring - 2)], ring_send)
+    arrived(w_all.at[pl.ds(0, ring - 1)], pair_send)
+    for sent in (tail_send, tail_pair_send):
+        arrived(w_all.at[0, :, pl.ds(0, 2 * (TAIL - 1) * short), :], sent.at[0])
+        arrived(w_all.at[0, :, pl.ds(0, 2 * short), pl.ds(0, shared)], sent.at[1])
+    arrived(w_all.at[pl.ds(0, 4), :, pl.ds(0, short), pl.ds(0, depth - shared)], end_send)
     arrived(table.at[pl.ds(0, 1 + 2 * (2 * half - 1))], coef_send)
     total = stage[pb]
     arrived(landed.at[pl.ds(0, transfers - 1)], sum_recv)
@@ -353,12 +415,17 @@
             dma(()),
             dma(((half - 1) * CHUNKS + TAIL,)),
             dma(()),
+            dma((2,)),
+            dma((2,)),
+            dma(()),
+            dma(()),
             dma(()),
             dma((2, half)),
             dma(()),
             dma(()),
             dma(()),
-            pltpu.SemaphoreType.REGULAR((rounds_of(transfers),)),
+            pltpu.SemaphoreType.REGULAR((2,)),
+            pltpu.SemaphoreType.REGULAR,
         ],
         compiler_params=pltpu.CompilerParams(
             collective_id=0, has_side_effects=True, vmem_limit_bytes=40 * 1024 * 1024

time: 98.8 us -> 97.9 us (level)
  no operation moved by 1% of the time
where the time goes in v4:
time: 97.9 us; the launch traced here: 97.8 us
  Pallas kernels  97.2 us (99%)
    pallas_call x1, Pallas kernels, body(): pl.pallas_call(functools.partial(kernel, ring, transfers), out_shape=jax....  97.2 us

profile of v4, /device:TPU:1, one launch (start us, length us, event | category | flops | bytes accessed | tf_op | source)
XLA Modules:
  0.0 97.8 jit_solution(3939895738827810972)
XLA Ops:
  0.0 97.2 %shard_map.64 = f32[4,2,256]{2,1,0:T(2,128)S(1)} custom-call(bf16[1,2,128,2048]{3,2,1,0:T(8,128)(2,1)} %w_hbm.1, bf16[768,2048]{1,0:T(8,128)(2,1)} %bitcast.5, bf16[6,128,2048]{2,1,0:T(8,128)(2,1)} %bitcast.6, s32[1,6]{1,0:T(1,128)} %bitcast.8, s32[1,6]{1,0:T(1,128)} %bitcast.9, f32[2,4]{1,0:T(2,128)} %bitcast.7), custom_call_target="tpu_custom_call" | custom-call | flops 12884901888 | bytes 8388608 | tf_op jit(solution)/shard_map/pallas_call | solution.py:393
  97.2 0.6 copy.8

commit v5 on v4

--- a/solution.py
+++ b/solution.py
@@ -11,6 +11,7 @@
 CHUNKS = 4
 FLIGHT = 2
 TAIL = 4
+REUSE = 6
 DIRECT = 4
 UP, DOWN = 0, 1
 
@@ -85,7 +86,7 @@
         block = 2 * level(direction, hop) + core
         return pltpu.make_async_remote_copy(
             src_ref=piece(block, index), dst_ref=piece(block, index),
-            send_sem=ring_send, recv_sem=ring_recv.at[direction, number],
+            send_sem=ring_send, recv_sem=ring_recv.at[direction, number % REUSE],
             device_id={"kb": up if direction == UP else down}, device_id_type=MESH,
         )
 
@@ -93,7 +94,7 @@
         index = place(direction, number)
         return pltpu.make_async_remote_copy(
             src_ref=w_hbm.at[0, :, pl.ds(index * chunk, chunk), :], dst_ref=piece(kb, index),
-            send_sem=ring_send, recv_sem=ring_recv.at[direction, number],
+            send_sem=ring_send, recv_sem=ring_recv.at[direction, number % REUSE],
             device_id={"kb": up if direction == UP else down}, device_id_type=MESH,
         )
 
@@ -107,26 +108,28 @@
         block = 2 * level(direction, half - 1 + src_hop) + core
         part = w_all.at[block, :, pl.ds(tail_place(direction, at), short), pl.ds(0, lanes)]
         return remote(
-            part, part, send_sem, ring_recv.at[direction, full + at], {"kb": up if direction == UP else down}
+            part, part, send_sem, ring_recv.at[direction, REUSE + at], {"kb": up if direction == UP else down}
         )
 
     def tail_pair(direction, at, lanes=depth, send_sem=tail_pair_send.at[0]):
         block = 2 * level(direction, half) + core
         part = w_all.at[block, :, pl.ds(tail_place(direction, at), short), pl.ds(0, lanes)]
-        return remote(part, part, send_sem, pair_recv.at[full + at], {"kb": sibling})
-
-    def end_copy(direction, to_core):
-        block = 2 * level(direction, half - 1) + core
+        return remote(part, part, send_sem, pair_recv.at[(full + at) % 2], {"kb": sibling})
+
+    def end_copy(direction, by, to_core):
+        block = 2 * level(by, half - 1) + core
         part = w_all.at[block, :, pl.ds(tail_place(direction, TAIL - 1), short), pl.ds(shared, depth - shared)]
-        chip = up - core if direction == UP else down - core
-        return remote(part, part, end_send, end_recv, {"kb": chip + to_core})
+        chip = up - core if by == UP else down - core
+        return remote(part, part, end_send.at[direction], end_recv, {"kb": chip + to_core})
+
+    end_less, end_more = z == ring - 1, z == 1
 
     def pair(direction, number, owner):
         hop, index = number // CHUNKS + 1, place(direction, number % CHUNKS)
         block = 2 * level(direction, hop) + owner
         return pltpu.make_async_remote_copy(
             src_ref=piece(block, index), dst_ref=piece(block, index),
-            send_sem=pair_send, recv_sem=pair_recv.at[number],
+            send_sem=pair_send, recv_sem=pair_recv.at[number % 2],
             device_id={"kb": sibling}, device_id_type=MESH,
         )
 
@@ -195,25 +198,53 @@
         ))
     ]
     barrier = pltpu.get_barrier_semaphore()
-    for other in (down, sibling):
-        pl.semaphore_signal(barrier, inc=1, device_id={"kb": other}, device_id_type=MESH)
+
+    def first_out(direction):
+        for number in range(FLIGHT):
+            first_copy(direction, number).start()
+
+    above_is_nearer, below_is_nearer = z >= half, (z > 0) & (z <= half)
+
+    @pl.when(jnp.logical_not(above_is_nearer))
+    def _():
+        pl.semaphore_signal(barrier, inc=1, device_id={"kb": up}, device_id_type=MESH)
+
+    @pl.when(jnp.logical_not(below_is_nearer))
+    def _():
+        pl.semaphore_signal(barrier, inc=1, device_id={"kb": down}, device_id_type=MESH)
+
+    pl.semaphore_signal(barrier, inc=1, device_id={"kb": sibling}, device_id_type=MESH)
 
     @pl.when(z == 0)
     def _():
         for other in plane:
             pl.semaphore_signal(barrier, inc=1, device_id={"pb": other}, device_id_type=MESH)
 
-    pl.semaphore_wait(barrier, jnp.where(z == 0, 2 + len(plane), 2))
-
-    pl.semaphore_signal(joined, inc=1, device_id={"kb": up}, device_id_type=MESH)
-    for number in range(FLIGHT):
-        first_copy(UP, number).start()
+    pl.semaphore_wait(barrier, jnp.where(z == 0, 1 + len(plane), jnp.where(z == half, 3, 2)))
+
+    @pl.when(above_is_nearer)
+    def _():
+        pl.semaphore_signal(joined.at[DOWN], inc=1, device_id={"kb": up}, device_id_type=MESH)
+        first_out(UP)
+
+    @pl.when(below_is_nearer)
+    def _():
+        pl.semaphore_signal(joined.at[UP], inc=1, device_id={"kb": down}, device_id_type=MESH)
+        first_out(DOWN)
+
     own_pair(kb).start()
     for load in loads:
         load.start()
-    pl.semaphore_wait(joined, 1)
-    for number in range(FLIGHT):
-        first_copy(DOWN, number).start()
+
+    @pl.when(jnp.logical_not(above_is_nearer))
+    def _():
+        pl.semaphore_wait(joined.at[UP], 1)
+        first_out(UP)
+
+    @pl.when(jnp.logical_not(below_is_nearer))
+    def _():
+        pl.semaphore_wait(joined.at[DOWN], 1)
+        first_out(DOWN)
 
     table[kb] = jnp.zeros_like(table[0])
     loads[0].wait()
@@ -249,20 +280,14 @@
                 def _():
                     ring_copy(direction, later, 0).start()
 
-                @pl.when((later >= full) & (later < full + CHUNKS // 2))
+                @pl.when(later == full)
                 def _():
-                    for i in range(chunk // short):
-                        piece_at = (later - full) * (chunk // short) + i
-
-                        @pl.when(piece_at < TAIL - 1)
-                        def _():
-                            tail_copy(direction, piece_at, 0).start()
-
-                @pl.when(later == full + CHUNKS // 2 - 1)
+                    tail_copy(direction, 0, 0).start()
+
+                @pl.when(later == full + 1)
                 def _():
-                    tail_copy(direction, TAIL - 1, 0, shared, tail_send.at[1]).start()
-                    end_copy(direction, core).start()
-                    end_copy(direction, 1 - core).start()
+                    for at in range(1, TAIL - 1):
+                        tail_copy(direction, at, 0).start()
 
                 pair(direction, number, core).start()
 
@@ -286,7 +311,7 @@
 
         @pl.when(hop > 0)
         def _():
-            arrived(w_all.at[pl.ds(0, 2), :, pl.ds(0, chunk), :], pair_recv.at[number])
+            arrived(w_all.at[pl.ds(0, 2), :, pl.ds(0, chunk), :], pair_recv.at[number % 2])
 
         make_image(chunk, [
             (2 * level(direction, hop) + owner, at_row, buffer, owner * rows + at_row)
@@ -322,20 +347,42 @@
         chosen = jnp.sum(chosen, axis=1, keepdims=True)
         picked[2 * s : 2 * s + 2, :] = jnp.broadcast_to(chosen[0:2, :], (2, picked.shape[1]))
 
+    def send_end(direction):
+        end_copy(direction, direction, core).start()
+
+        @pl.when(jnp.logical_not(end_less) | (direction == DOWN))
+        def _():
+            end_copy(direction, direction, 1 - core).start()
+
+        if direction == DOWN:
+
+            @pl.when(end_more)
+            def _():
+                end_copy(UP, DOWN, 1 - core).start()
+
     def last_step(at, carry):
-        @pl.when(at < TAIL - 1)
+        @pl.when(at == 0)
+        def _():
+            for direction in (UP, DOWN):
+                tail_copy(direction, 0, 1).wait_recv()
+                tail_copy(direction, TAIL - 1, 0, shared, tail_send.at[1]).start()
+                tail_pair(direction, 0).start()
+            arrived(w_all.at[pl.ds(0, 2), :, pl.ds(0, short), :], pair_recv.at[full % 2])
+
+        @pl.when((at > 0) & (at < TAIL - 1))
         def _():
             for direction in (UP, DOWN):
                 tail_copy(direction, at, 1).wait_recv()
+                pl.when(at == 1)(lambda direction=direction: send_end(direction))
                 tail_pair(direction, at).start()
-            arrived(w_all.at[pl.ds(0, 2), :, pl.ds(0, short), :], pair_recv.at[full + at])
+            arrived(w_all.at[pl.ds(0, 2), :, pl.ds(0, short), :], pair_recv.at[(full + at) % 2])
 
         @pl.when(at == TAIL - 1)
         def _():
             for direction in (UP, DOWN):
                 tail_copy(direction, TAIL - 1, 1, shared).wait_recv()
                 tail_pair(direction, TAIL - 1, shared, tail_pair_send.at[1]).start()
-            arrived(w_all.at[pl.ds(0, 2), :, pl.ds(0, short), pl.ds(0, shared)], pair_recv.at[full + TAIL - 1])
+            arrived(w_all.at[pl.ds(0, 2), :, pl.ds(0, short), pl.ds(0, shared)], pair_recv.at[(full + TAIL - 1) % 2])
             arrived(w_all.at[pl.ds(0, 4), :, pl.ds(0, short), pl.ds(0, depth - shared)], end_recv)
 
         make_image(short, [
@@ -366,7 +413,17 @@
     for sent in (tail_send, tail_pair_send):
         arrived(w_all.at[0, :, pl.ds(0, 2 * (TAIL - 1) * short), :], sent.at[0])
         arrived(w_all.at[0, :, pl.ds(0, 2 * short), pl.ds(0, shared)], sent.at[1])
-    arrived(w_all.at[pl.ds(0, 4), :, pl.ds(0, short), pl.ds(0, depth - shared)], end_send)
+    end_lanes = pl.ds(0, depth - shared)
+    arrived(w_all.at[pl.ds(0, 2), :, pl.ds(0, short), end_lanes], end_send.at[DOWN])
+
+    for sent, condition in (
+        (1, end_less), (2, jnp.logical_not(end_less) & jnp.logical_not(end_more)), (3, end_more)
+    ):
+
+        @pl.when(condition)
+        def _(sent=sent):
+            arrived(w_all.at[pl.ds(0, sent), :, pl.ds(0, short), end_lanes], end_send.at[UP])
+
     arrived(table.at[pl.ds(0, 1 + 2 * (2 * half - 1))], coef_send)
     total = stage[pb]
     arrived(landed.at[pl.ds(0, transfers - 1)], sum_recv)
@@ -411,13 +468,13 @@
             pltpu.VMEM((2, local_k), jnp.float32),
             dma((6,)),
             dma(()),
-            dma((2, (half - 1) * CHUNKS + TAIL)),
-            dma(()),
-            dma(((half - 1) * CHUNKS + TAIL,)),
+            dma((2, REUSE + TAIL)),
+            dma(()),
+            dma((2,)),
             dma(()),
             dma((2,)),
             dma((2,)),
-            dma(()),
+            dma((2,)),
             dma(()),
             dma(()),
             dma((2, half)),
@@ -425,7 +482,7 @@
             dma(()),
             dma(()),
             pltpu.SemaphoreType.REGULAR((2,)),
-            pltpu.SemaphoreType.REGULAR,
+            pltpu.SemaphoreType.REGULAR((2,)),
         ],
         compiler_params=pltpu.CompilerParams(
             collective_id=0, has_side_effects=True, vmem_limit_bytes=40 * 1024 * 1024

time: 97.9 us -> 97.7 us (level)
  no operation moved by 1% of the time
where the time goes in v5:
time: 97.7 us; the launch traced here: 97.6 us
  Pallas kernels  97 us (99%)
    pallas_call x1, Pallas kernels, body(): pl.pallas_call(functools.partial(kernel, ring, transfers), out_shape=jax....  97 us

profile of v5, /device:TPU:1, one launch (start us, length us, event | category | flops | bytes accessed | tf_op | source)
XLA Modules:
  0.0 97.6 jit_solution(13353287389539161227)
XLA Ops:
  0.0 97.0 %shard_map.64 = f32[4,2,256]{2,1,0:T(2,128)S(1)} custom-call(bf16[1,2,128,2048]{3,2,1,0:T(8,128)(2,1)} %w_hbm.1, bf16[768,2048]{1,0:T(8,128)(2,1)} %bitcast.5, bf16[6,128,2048]{2,1,0:T(8,128)(2,1)} %bitcast.6, s32[1,6]{1,0:T(1,128)} %bitcast.8, s32[1,6]{1,0:T(1,128)} %bitcast.9, f32[2,4]{1,0:T(2,128)} %bitcast.7), custom_call_target="tpu_custom_call" | custom-call | flops 12884901888 | bytes 8388608 | tf_op jit(solution)/shard_map/pallas_call | solution.py:450
  97.0 0.6 copy.8

commit v6 on v5

--- a/solution.py
+++ b/solution.py
@@ -29,7 +29,7 @@
     ring, transfers, w_hbm, val_hbm, cond_hbm, first_hbm, second_hbm, coef_hbm, out_ref,
     w_all, val, val_t, cond, image, acc, table, picked, stage, landed, first, second, coef,
     local_sem, ring_send, ring_recv, pair_send, pair_recv, own_recv, tail_send, tail_pair_send, end_send, end_recv,
-    coef_send, coef_recv, coef_pair_recv, sum_send, sum_recv, known, joined,
+    coef_send, coef_recv, coef_pair_recv, sum_send, sum_recv, known, joined, met,
 ):
     half = ring // 2
     rows = w_hbm.shape[2]
@@ -213,14 +213,16 @@
     def _():
         pl.semaphore_signal(barrier, inc=1, device_id={"kb": down}, device_id_type=MESH)
 
-    pl.semaphore_signal(barrier, inc=1, device_id={"kb": sibling}, device_id_type=MESH)
+    @pl.when(core == 1)
+    def _():
+        pl.semaphore_signal(barrier, inc=1, device_id={"kb": sibling}, device_id_type=MESH)
 
     @pl.when(z == 0)
     def _():
         for other in plane:
             pl.semaphore_signal(barrier, inc=1, device_id={"pb": other}, device_id_type=MESH)
 
-    pl.semaphore_wait(barrier, jnp.where(z == 0, 1 + len(plane), jnp.where(z == half, 3, 2)))
+    pl.semaphore_wait(barrier, jnp.where(z == 0, len(plane), jnp.where(z == half, 2, 1)) + 1 - core)
 
     @pl.when(above_is_nearer)
     def _():
@@ -232,7 +234,10 @@
         pl.semaphore_signal(joined.at[UP], inc=1, device_id={"kb": down}, device_id_type=MESH)
         first_out(DOWN)
 
-    own_pair(kb).start()
+    @pl.when(core == 0)
+    def _():
+        pl.semaphore_signal(met, inc=1, device_id={"kb": sibling}, device_id_type=MESH)
+
     for load in loads:
         load.start()
 
@@ -245,6 +250,12 @@
     def _():
         pl.semaphore_wait(joined.at[DOWN], 1)
         first_out(DOWN)
+
+    @pl.when(core == 1)
+    def _():
+        pl.semaphore_wait(met, 1)
+
+    own_pair(kb).start()
 
     table[kb] = jnp.zeros_like(table[0])
     loads[0].wait()
@@ -483,6 +494,7 @@
             dma(()),
             pltpu.SemaphoreType.REGULAR((2,)),
             pltpu.SemaphoreType.REGULAR((2,)),
+            pltpu.SemaphoreType.REGULAR,
         ],
         compiler_params=pltpu.CompilerParams(
             collective_id=0, has_side_effects=True, vmem_limit_bytes=40 * 1024 * 1024

time: 97.7 us -> 97.3 us (level)
  no operation moved by 1% of the time
where the time goes in v6:
time: 97.3 us; the launch traced here: 97.2 us
  Pallas kernels  96.6 us (99%)
    pallas_call x1, Pallas kernels, body(): pl.pallas_call(functools.partial(kernel, ring, transfers), out_shape=jax....  96.6 us

profile of v6, /device:TPU:1, one launch (start us, length us, event | category | flops | bytes accessed | tf_op | source)
XLA Modules:
  0.0 97.2 jit_solution(4902629412757495738)
XLA Ops:
  0.0 96.6 %shard_map.64 = f32[4,2,256]{2,1,0:T(2,128)S(1)} custom-call(bf16[1,2,128,2048]{3,2,1,0:T(8,128)(2,1)} %w_hbm.1, bf16[768,2048]{1,0:T(8,128)(2,1)} %bitcast.5, bf16[6,128,2048]{2,1,0:T(8,128)(2,1)} %bitcast.6, s32[1,6]{1,0:T(1,128)} %bitcast.8, s32[1,6]{1,0:T(1,128)} %bitcast.9, f32[2,4]{1,0:T(2,128)} %bitcast.7), custom_call_target="tpu_custom_call" | custom-call | flops 12884901888 | bytes 8388608 | tf_op jit(solution)/shard_map/pallas_call | solution.py:461
  96.6 0.6 copy.8
